TPU v7x, 256 devices: a whole 4x4x8 slice. The times are simulated.
256 devices in a mesh: dp: 64 (over x, z, core), expert: 4 (over y).
Axes of the slice: x: 4, y: 4, z: 8, core: 2. Of those that a mesh axis runs over, the one named last changes fastest.
Arguments:
- grad: bfloat16 [16, 7168, 2048], P('expert', 'dp')
- momentum: float32 [16, 7168, 2048], P('expert', 'dp'), may hold values from -6 to 6
- placement: int32 [16], replicated, may hold values from 0 to 15, as said below
Outputs:
- momentum_new: float32 [16, 7168, 2048], P('expert', 'dp')
- update: bfloat16 [16, 7168, 2048], P('expert', 'dp')
Inputs may be any that keep to these rules, and one draw needn't show every extreme that they name: placement is a permutation; position e lies in group e // 4, and placement[e] // 4 is the new group. The 4 experts of each group go to 4 different groups, so every group receives exactly one expert from every group.
All inputs are finite; a program needn't handle non-finite values.
Results may differ from a plain program's by a relative error of at most 0.0074.
Values may be sent and summed in bfloat16 or wider, within the bound.
A program may use at most 128 MiB of HBM per device.

v0:
```python
import math

import jax
import jax.numpy as jnp
from jax import lax
from jax.sharding import PartitionSpec as P

D = 7168


def from_partner(value, axis, stride):
    mask = 2**stride
    pairs = [(source, source ^ mask) for source in range(lax.axis_size(axis))]
    return lax.ppermute(value, axis, pairs)


def split_pair(gram_part, member, level):
    half_rows = gram_part.shape[0] // 2
    upper = member >> level & 1 == 1
    lower_half = gram_part[:half_rows]
    upper_half = gram_part[half_rows:]
    kept_half = jnp.where(upper, upper_half, lower_half)
    given_half = jnp.where(upper, lower_half, upper_half)
    return (kept_half, given_half)


def join_pair(gram_part, other_half, member, level):
    upper = member >> level & 1 == 1
    return jnp.where(
        upper,
        jnp.concatenate([other_half, gram_part], axis=0),
        jnp.concatenate([gram_part, other_half], axis=0),
    )


def reduce_halves(gram_part, swap_bits, member):
    for level in range(len(swap_bits)):
        kept_half, given_half = split_pair(gram_part, member, level)
        gram_part = kept_half + from_partner(given_half, "dp", swap_bits[level])
    return gram_part


def collect_halves(gram_part, swap_bits, member):
    for level in reversed(range(len(swap_bits))):
        other_half = from_partner(gram_part, "dp", swap_bits[level])
        gram_part = join_pair(gram_part, other_half, member, level)
    return gram_part


def shards(grad, momentum, placement):
    local_count = grad.shape[0]
    row_count = grad.shape[1]
    columns = grad.shape[2]
    dp_count = lax.axis_size("dp")
    group_size = dp_count // local_count
    piece_rows = row_count // group_size
    my_group = lax.axis_index("expert")
    my_index = lax.axis_index("dp")
    momentum_new = 0.95 * momentum + grad.astype(jnp.float32)
    moved = momentum_new.astype(jnp.bfloat16)
    slot_ids = lax.iota(jnp.int32, local_count)
    my_targets = (
        lax.dynamic_slice_in_dim(placement, my_group * local_count, local_count) // local_count
    )
    choose = (my_targets[None, :] == slot_ids[:, None]).astype(jnp.int32)
    send_slot = jnp.sum(choose * slot_ids[None, :], axis=1)
    outgoing = jnp.take(moved, send_slot, axis=0)
    arrived = lax.all_to_all(outgoing, "expert", split_axis=0, concat_axis=0, tiled=True)
    moves_table = placement.reshape(local_count, local_count)
    into_mine = moves_table // local_count == my_group
    new_slot = jnp.sum(jnp.where(into_mine, moves_table % local_count, 0), axis=1)
    picker = (new_slot[None, :] == slot_ids[:, None]).astype(jnp.int32)
    from_source = jnp.sum(picker * slot_ids[None, :], axis=1)
    by_block = jnp.take(arrived, from_source, axis=0)
    pieces = by_block.reshape(local_count, group_size, piece_rows, columns)
    outgoing_rows = pieces.reshape(local_count * group_size, piece_rows, columns)
    block_id = my_index // group_size
    member = my_index % group_size
    first_bit = 0
    swap_bits = [first_bit + level for level in range(group_size.bit_length() - 1)]
    received = lax.all_to_all(outgoing_rows, "dp", split_axis=0, concat_axis=0, tiled=True)
    owned_rows = received.reshape(dp_count * piece_rows, columns)
    values = owned_rows.astype(jnp.float32)
    partial_value = jnp.sum(values * values)
    in_block = (slot_ids == block_id).astype(jnp.float32)
    totals = lax.psum(partial_value * in_block, "dp")
    squares = jnp.sum(totals * in_block)
    factor = 0.5 * math.sqrt(columns) / jnp.sqrt(squares + 1e-06)
    normal = (values * factor).astype(jnp.bfloat16)
    gram_part = lax.dot_general(
        normal, normal, (((0,), (0,)), ((), ())), preferred_element_type=jnp.float32
    )
    gram_part = reduce_halves(gram_part, swap_bits, member)
    gram_whole = collect_halves(gram_part.astype(jnp.bfloat16), swap_bits, member)
    product = jnp.dot(normal, gram_whole, preferred_element_type=jnp.float32).astype(jnp.bfloat16)
    second = jnp.dot(product, gram_whole, preferred_element_type=jnp.float32)
    orthogonal = (
        3.4445 * normal.astype(jnp.float32) - 4.775 * product.astype(jnp.float32) + 2.0315 * second
    )
    result = (orthogonal * math.sqrt(D)).astype(jnp.bfloat16)
    returned = lax.all_to_all(
        result.reshape(dp_count, piece_rows, columns), "dp", split_axis=0, concat_axis=0, tiled=True
    )
    ordered = returned.reshape(local_count, group_size, piece_rows, columns)
    update = ordered.reshape(local_count, row_count, columns)
    return (momentum_new, update)


def solution(mesh):
    return jax.shard_map(
        shards,
        mesh=mesh,
        in_specs=(P("expert", "dp", None), P("expert", "dp", None), P()),
        out_specs=(P("expert", "dp", None), P("expert", "dp", None)),
        check_vma=False,
    )
```

profile of v0, /device:TPU:1, one launch (start us, length us, event | category | flops | bytes accessed | tf_op | source)
XLA Modules:
  0.0 743.9 jit_solution(13957444276365384360)
XLA Ops:
  0.6 0.7 and_select_fusion
  1.4 0.1 select_reduce_fusion.1
  1.5 6.0 fusion.9
  7.5 2.2 gather_fusion
  9.7 0.0 copy-start.5
  9.7 1.5 broadcast_select_fusion.1
  11.2 5.0 all-to-all-start
  16.2 0.0 copy-done.5
  16.2 0.1 reshape.24
  16.3 0.1 fusion.4
  16.4 0.1 select_reduce_fusion
  16.5 21.4 %all-to-all-done = bf16[4,112,2048]{2,1,0:T(8,128)(2,1)S(1)} async-done(((bf16[4,112,2048]{2,1,0:T(8,128)(2,1)}), bf16[4,112,2048]{2,1,0:T(8,128)(2,1)S(1)}, u32[]{:S(2)}, u32[]{:S(2)}) %all-to-all-start) | async-done | bytes 1835040 | tf_op jit(solution)/shard_map/all_to_all | solution.py:68
  37.9 1.9 gather_fusion.1
  39.8 1.7 broadcast_select_fusion
  41.6 1.7 reshape_reshape.6
  43.2 14.2 %all-to-all-start.1 = ((bf16[64,7,2048]{2,1,0:T(8,128)(2,1)}), bf16[64,7,2048]{2,1,0:T(8,128)(2,1)S(1)}, u32[]{:S(2)}, u32[]{:S(2)}) async-start(bf16[64,7,2048]{2,1,0:T(8,128)(2,1)} %reshape_reshape.6), calls=%async_computation.1 | async-start | bytes 4194304 | tf_op jit(solution)/shard_map/all_to_all | solution.py:81
  57.5 51.2 %all-to-all-done.1 = bf16[64,7,2048]{2,1,0:T(8,128)(2,1)S(1)} async-done(((bf16[64,7,2048]{2,1,0:T(8,128)(2,1)}), bf16[64,7,2048]{2,1,0:T(8,128)(2,1)S(1)}, u32[]{:S(2)}, u32[]{:S(2)}) %all-to-all-start.1) | async-done | bytes 1835040 | tf_op jit(solution)/shard_map/all_to_all | solution.py:81
  108.7 1.7 fusion
  110.4 0.6 compare_select_fusion.6
  111.0 123.8 %psum.7 = f32[4]{0:T(128)S(1)} all-reduce(f32[4]{0:T(128)S(1)} %compare_select_fusion.6), channel_id=1, replica_groups=mesh['dp'=64,'expert'=4] {'dp'}, use_global_device_ids=true, to_apply=%region_4.6 | all-reduce | flops 4 | bytes 32 | tf_op jit(solution)/shard_map/psum | solution.py:86
  234.8 0.6 fusion.6
  236.1 1.1 fusion.1
  237.3 0.0 copy-start.2
  237.3 1.2 copy-done.2
  238.5 8.1 %convolution_bitcast_fusion = f32[2048,2048]{1,0:T(8,128)} fusion(bf16[64,7,2048]{2,0,1:T(8,128)(2,1)S(1)} %fusion.1), kind=kOutput, calls=%fused_computation.2 | convolution fusion | flops 3758096384 | bytes 18612224 | tf_op jit(solution)/shard_map/dot_general | solution.py:90
  246.6 11.7 %slice_select_fusion = f32[1024,2048]{1,0:T(8,128)} fusion(f32[2048,2048]{1,0:T(8,128)} %convolution_bitcast_fusion, pred[]{:T(512)S(6)} %eq.68), kind=kLoop, calls=%fused_computation.5 | loop fusion | flops 2097152 | bytes 25165824 | tf_op jit(solution)/shard_map/jit(_where)/select_n | solution.py:23
  258.3 1.3 collective-permute-start
  259.6 13.1 %collective-permute-done = f32[1024,2048]{1,0:T(8,128)} collective-permute-done((f32[1024,2048]{1,0:T(8,128)}, f32[1024,2048]{1,0:T(8,128)}, u32[]{:S(2)}, u32[]{:S(2)}) %collective-permute-start) | collective-permute-done | bytes 8388640 | tf_op jit(solution)/shard_map/ppermute | solution.py:14
  272.7 9.6 %select_add_fusion = f32[1024,2048]{1,0:T(8,128)S(1)} fusion(f32[1024,2048]{1,0:T(8,128)} %collective-permute-done, f32[2048,2048]{1,0:T(8,128)} %convolution_bitcast_fusion, pred[]{:T(512)S(6)} %eq.68), kind=kLoop, calls=%fused_computation.4 | loop fusion | flops 4194304 | bytes 33554432 | tf_op jit(solution)/shard_map/add | solution.py:39
  282.3 0.0 copy-start
  282.3 3.1 slice_select_fusion.1
  285.4 1.3 copy-done
  286.8 0.0 collective-permute-start.1
  286.8 92.1 %collective-permute-done.1 = f32[512,2048]{1,0:T(8,128)} collective-permute-done((f32[512,2048]{1,0:T(8,128)}, f32[512,2048]{1,0:T(8,128)}, u32[]{:S(2)}, u32[]{:S(2)}) %collective-permute-start.1) | collective-permute-done | bytes 4194336 | tf_op jit(solution)/shard_map/ppermute | solution.py:14
  378.9 6.0 select_add_fusion.1
  384.9 0.0 copy-start.1
  384.9 1.9 copy-done.1
  386.8 0.3 slice_select_fusion.2
  387.1 0.1 collective-permute-start.2
  387.2 93.4 %collective-permute-done.2 = f32[256,2048]{1,0:T(8,128)} collective-permute-done((f32[256,2048]{1,0:T(8,128)S(1)}, f32[256,2048]{1,0:T(8,128)}, u32[]{:S(2)}, u32[]{:S(2)}) %collective-permute-start.2) | collective-permute-done | bytes 2097184 | tf_op jit(solution)/shard_map/ppermute | solution.py:14
  480.7 3.4 select_add_fusion.2
  484.1 0.1 slice_select_fusion.3
  484.2 0.1 collective-permute-start.3
  484.3 48.0 %collective-permute-done.3 = f32[128,2048]{1,0:T(8,128)S(1)} collective-permute-done((f32[128,2048]{1,0:T(8,128)S(1)}, f32[128,2048]{1,0:T(8,128)S(1)}, u32[]{:S(2)}, u32[]{:S(2)}) %collective-permute-start.3) | collective-permute-done | bytes 1048608 | tf_op jit(solution)/shard_map/ppermute | solution.py:14
  532.3 0.2 add_convert_fusion
  532.5 3.4 collective-permute-start.4
  535.9 22.3 %collective-permute-done.4 = bf16[128,2048]{1,0:T(8,128)(2,1)S(1)} collective-permute-done((bf16[128,2048]{1,0:T(8,128)(2,1)S(1)}, bf16[128,2048]{1,0:T(8,128)(2,1)S(1)}, u32[]{:S(2)}, u32[]{:S(2)}) %collective-permute-start.4) | collective-permute-done | bytes 524320 | tf_op jit(solution)/shard_map/ppermute | solution.py:14
  558.2 0.2 maximum_select_fusion.5
  558.5 0.1 collective-permute-start.5
  558.6 45.2 %collective-permute-done.5 = bf16[256,2048]{1,0:T(8,128)(2,1)S(1)} collective-permute-done((bf16[256,2048]{1,0:T(8,128)(2,1)S(1)}, bf16[256,2048]{1,0:T(8,128)(2,1)S(1)}, u32[]{:S(2)}, u32[]{:S(2)}) %collective-permute-start.5) | collective-permute-done | bytes 1048608 | tf_op jit(solution)/shard_map/ppermute | solution.py:14
  603.8 1.0 maximum_select_fusion.2
  604.8 0.0 copy-start.3
  604.8 0.1 collective-permute-start.6
  604.9 46.7 %collective-permute-done.6 = bf16[512,2048]{1,0:T(8,128)(2,1)S(1)} collective-permute-done((bf16[512,2048]{1,0:T(8,128)(2,1)S(1)}, bf16[512,2048]{1,0:T(8,128)(2,1)S(1)}, u32[]{:S(2)}, u32[]{:S(2)}) %collective-permute-start.6) | collective-permute-done | bytes 2097184 | tf_op jit(solution)/shard_map/ppermute | solution.py:14
  651.6 3.7 maximum_select_fusion.1
  655.3 1.3 collective-permute-start.7
  656.6 1.0 copy.8
  657.7 1.6 convert_element_type.43
  659.2 4.5 collective-permute-done.7
  663.8 8.5 %convolution_convert_fusion = bf16[448,2048]{1,0:T(8,128)(2,1)S(1)} fusion(bf16[448,2048]{1,0:T(8,128)(2,1)} %convert_element_type.43, bf16[1024,2048]{1,0:T(8,128)(2,1)} %maximum_select_fusion.1, bf16[1024,2048]{1,0:T(8,128)(2,1)} %collective-permute-done.7, pred[]{:T(512)S(6)} %eq.68), kind=kOutput, calls=%fused_computation.15 | convolution fusion | flops 3796762624 | bytes 12058625 | tf_op jit(solution)/shard_map/dot_general | solution.py:95
  672.3 9.3 %multiply_convert_fusion = bf16[448,2048]{1,0:T(8,128)(2,1)} fusion(bf16[448,2048]{1,0:T(8,128)(2,1)S(1)} %convolution_convert_fusion, bf16[448,2048]{1,0:T(8,128)(2,1)S(1)} %copy-done.4, bf16[1024,2048]{1,0:T(8,128)(2,1)} %maximum_select_fusion.1, bf16[1024,2048]{1,0:T(8,128)(2,1)} %collective-permute-done.7, pred[]{:T(512)S(6)} %eq.68), kind=kOutput, calls=%fused_computation.13 | convolution fusion | flops 3804102656 | bytes 13893633 | tf_op jit(solution)/shard_map/dot_general | solution.py:96
  681.5 2.5 reshape.25
  684.1 56.1 %all_to_all.15 = bf16[64,7,2048]{2,1,0:T(8,128)(2,1)} all-to-all(bf16[64,7,2048]{2,1,0:T(8,128)(2,1)S(1)} %reshape.25), channel_id=1, replica_groups=mesh['dp'=64,'expert'=4] {'dp'}, dimensions={0} | all-to-all | bytes 3670016 | tf_op jit(solution)/shard_map/all_to_all | solution.py:101
  740.2 3.7 reshape_reshape.7
  (9 shorter events, 0.0 us)
Async XLA Ops:
  9.7 6.5 copy-start.5
  11.2 26.8 %all-to-all-start = ((bf16[4,112,2048]{2,1,0:T(8,128)(2,1)}), bf16[4,112,2048]{2,1,0:T(8,128)(2,1)S(1)}, u32[]{:S(2)}, u32[]{:S(2)}) async-start(bf16[4,112,2048]{2,1,0:T(8,128)(2,1)} %broadcast_select_fusion.1), calls=%async_computation | async-start | bytes 3670016 | tf_op jit(solution)/shard_map/all_to_all | solution.py:68
  43.2 65.4 %all-to-all-start.1 = ((bf16[64,7,2048]{2,1,0:T(8,128)(2,1)}), bf16[64,7,2048]{2,1,0:T(8,128)(2,1)S(1)}, u32[]{:S(2)}, u32[]{:S(2)}) async-start(bf16[64,7,2048]{2,1,0:T(8,128)(2,1)} %reshape_reshape.6), calls=%async_computation.1 | async-start | bytes 4194304 | tf_op jit(solution)/shard_map/all_to_all | solution.py:81
  237.3 1.2 copy-start.2
  258.3 14.5 %collective-permute-start = (f32[1024,2048]{1,0:T(8,128)}, f32[1024,2048]{1,0:T(8,128)}, u32[]{:S(2)}, u32[]{:S(2)}) collective-permute-start(f32[1024,2048]{1,0:T(8,128)} %slice_select_fusion), channel_id=1, source_target_pairs={{0,4},{4,0},{8,12},{12,8},{16,20},{20,16},{24,28},{28,24},{32,36},... | collective-permute-start | bytes 25165832 | tf_op jit(solution)/shard_map/ppermute | solution.py:14
  282.3 4.5 copy-start
  286.8 92.1 %collective-permute-start.1 = (f32[512,2048]{1,0:T(8,128)}, f32[512,2048]{1,0:T(8,128)}, u32[]{:S(2)}, u32[]{:S(2)}) collective-permute-start(f32[512,2048]{1,0:T(8,128)} %slice_select_fusion.1), channel_id=1, source_target_pairs={{0,8},{4,12},{8,0},{12,4},{16,24},{20,28},{24,16},{28,20},{32,40},... | collective-permute-start | bytes 12582920 | tf_op jit(solution)/shard_map/ppermute | solution.py:14
  384.9 1.9 copy-start.1
  387.1 93.5 %collective-permute-start.2 = (f32[256,2048]{1,0:T(8,128)S(1)}, f32[256,2048]{1,0:T(8,128)}, u32[]{:S(2)}, u32[]{:S(2)}) collective-permute-start(f32[256,2048]{1,0:T(8,128)S(1)} %slice_select_fusion.2), channel_id=1, source_target_pairs={{0,16},{4,20},{8,24},{12,28},{16,0},{20,4},{24,8},{28,12},{32,48},... | collective-permute-start | bytes 6291464 | tf_op jit(solution)/shard_map/ppermute | solution.py:14
  484.2 48.1 %collective-permute-start.3 = (f32[128,2048]{1,0:T(8,128)S(1)}, f32[128,2048]{1,0:T(8,128)S(1)}, u32[]{:S(2)}, u32[]{:S(2)}) collective-permute-start(f32[128,2048]{1,0:T(8,128)S(1)} %slice_select_fusion.3), channel_id=1, source_target_pairs={{0,32},{4,36},{8,40},{12,44},{16,48},{20,52},{24,56},{28,60},{32,0... | collective-permute-start | bytes 3145736 | tf_op jit(solution)/shard_map/ppermute | solution.py:14
  532.5 25.8 %collective-permute-start.4 = (bf16[128,2048]{1,0:T(8,128)(2,1)S(1)}, bf16[128,2048]{1,0:T(8,128)(2,1)S(1)}, u32[]{:S(2)}, u32[]{:S(2)}) collective-permute-start(bf16[128,2048]{1,0:T(8,128)(2,1)S(1)} %add_convert_fusion), channel_id=1, source_target_pairs={{0,32},{4,36},{8,40},{12,44},{16,48},{20,52},{24,56},{28,60},{32,0... | collective-permute-start | bytes 1572872 | tf_op jit(solution)/shard_map/ppermute | solution.py:14
  558.5 45.3 %collective-permute-start.5 = (bf16[256,2048]{1,0:T(8,128)(2,1)S(1)}, bf16[256,2048]{1,0:T(8,128)(2,1)S(1)}, u32[]{:S(2)}, u32[]{:S(2)}) collective-permute-start(bf16[256,2048]{1,0:T(8,128)(2,1)S(1)} %maximum_select_fusion.5), channel_id=1, source_target_pairs={{0,16},{4,20},{8,24},{12,28},{16,0},{20,4},{24,8},{28,12},{32,48},... | collective-permute-start | bytes 3145736 | tf_op jit(solution)/shard_map/ppermute | solution.py:14
  604.8 51.8 %copy-start.3 = (bf16[64,7,2048]{2,0,1:T(8,128)(2,1)S(1)}, bf16[64,7,2048]{2,0,1:T(8,128)(2,1)}, u32[]{:S(2)}) copy-start(bf16[64,7,2048]{2,0,1:T(8,128)(2,1)} %copy-done.2) | copy-start | bytes 5505028
  604.8 46.8 %collective-permute-start.6 = (bf16[512,2048]{1,0:T(8,128)(2,1)S(1)}, bf16[512,2048]{1,0:T(8,128)(2,1)S(1)}, u32[]{:S(2)}, u32[]{:S(2)}) collective-permute-start(bf16[512,2048]{1,0:T(8,128)(2,1)S(1)} %maximum_select_fusion.2), channel_id=1, source_target_pairs={{0,8},{4,12},{8,0},{12,4},{16,24},{20,28},{24,16},{28,20},{32,40},... | collective-permute-start | bytes 6291464 | tf_op jit(solution)/shard_map/ppermute | solution.py:14
  655.3 8.5 %collective-permute-start.7 = (bf16[1024,2048]{1,0:T(8,128)(2,1)}, bf16[1024,2048]{1,0:T(8,128)(2,1)}, u32[]{:S(2)}, u32[]{:S(2)}) collective-permute-start(bf16[1024,2048]{1,0:T(8,128)(2,1)} %maximum_select_fusion.1), channel_id=1, source_target_pairs={{0,4},{4,0},{8,12},{12,8},{16,20},{20,16},{24,28},{28,24},{32,36},... | collective-permute-start | bytes 12582920 | tf_op jit(solution)/shard_map/ppermute | solution.py:14
  659.2 13.1 %copy-start.4 = (bf16[448,2048]{1,0:T(8,128)(2,1)S(1)}, bf16[448,2048]{1,0:T(8,128)(2,1)}, u32[]{:S(2)}) copy-start(bf16[448,2048]{1,0:T(8,128)(2,1)} %convert_element_type.43) | copy-start | bytes 5505028
where the time goes:
time: 744 us
  waiting for transfers between devices  438 us (59%)
  blocking collectives  180 us (24%)
  other arithmetic  53.7 us (7%)
  matrix products  25.9 us (3%)
  starting transfers between devices  25.7 us (3%)
  local copies, waits for them, and re-layouts  19.1 us (3%)
    ppermute x8, waiting for transfers between devices, from_partner(): return lax.ppermute(value, axis, pairs)  365 us
    psum x1, blocking collectives, shards(): totals = lax.psum(partial_value * in_block, 'dp')  124 us
    all_to_all x1, blocking collectives, shards(): lax.all_to_all(result.reshape(dp_count, piece_rows, columns), 'dp', split...  56.1 us
    all_to_all x1, waiting for transfers between devices, shards(): lax.all_to_all(outgoing_rows, 'dp', split_axis=0, concat_axis=0, tiled=True)  51.2 us
    all_to_all x1, waiting for transfers between devices, shards(): lax.all_to_all(outgoing, 'expert', split_axis=0, concat_axis=0, tiled=True)  21.4 us
    add x3, other arithmetic, reduce_halves(): gram_part = kept_half + from_partner(given_half, 'dp', swap_bits[level])  19 us
    select_n x4, other arithmetic, split_pair(): given_half = jnp.where(upper, lower_half, upper_half)  15.2 us
  transfers between devices with their start and end apart: 10, of which 10 were waited for; matrix products, arithmetic and copies ran while one was open for 0% of the time, Pallas kernels for 0%

commit v1 on v0

v1 whole, which is shorter than its diff:
```python
import functools
import math

import jax
import jax.numpy as jnp
from jax import lax
from jax.experimental import pallas as pl
from jax.experimental.pallas import tpu as pltpu
from jax.sharding import PartitionSpec as P

D = 7168
MESH = pl.DeviceIdType.MESH
LOCAL = 4
RING = 8
ROWS = 112
OWNED = LOCAL * ROWS
FF = 2048
CHUNK = FF // RING
HALF = CHUNK // 2
WIDE = LOCAL * CHUNK
STRIP = WIDE + HALF
PART = HALF // 2


def prep_kernel(slots_ref, grad_ref, momentum_ref, new_ref, out_ref):
    new = 0.95 * momentum_ref[0] + grad_ref[0].astype(jnp.float32)
    new_ref[0] = new
    moved = new.astype(jnp.bfloat16)
    for q in range(out_ref.shape[0]):
        out_ref[q, 0] = moved[:, q * CHUNK : (q + 1) * CHUNK]


def prepare(slots, grad, momentum):
    halves = 2
    columns = FF // halves
    taken = pl.BlockSpec((1, ROWS, columns), lambda i, h, slots: (slots[i], 0, h))
    return pl.pallas_call(
        prep_kernel,
        grid_spec=pltpu.PrefetchScalarGridSpec(
            num_scalar_prefetch=1,
            grid=(LOCAL, halves),
            in_specs=[taken, taken],
            out_specs=[
                taken,
                pl.BlockSpec((RING // halves, 1, ROWS, CHUNK), lambda i, h, slots: (h, i, 0, 0)),
            ],
        ),
        out_shape=[
            jax.ShapeDtypeStruct((LOCAL, ROWS, FF), jnp.float32),
            jax.ShapeDtypeStruct((RING, LOCAL, ROWS, CHUNK), jnp.bfloat16),
        ],
        compiler_params=pltpu.CompilerParams(vmem_limit_bytes=32 << 20),
        name="prepare",
    )(slots, grad, momentum)


def place_kernel(sources_ref, from_ref, to_ref):
    to_ref[...] = from_ref[...]


def place(sources, returned):
    return pl.pallas_call(
        place_kernel,
        grid_spec=pltpu.PrefetchScalarGridSpec(
            num_scalar_prefetch=1,
            grid=(LOCAL,),
            in_specs=[pl.BlockSpec((1, ROWS, FF), lambda i, sources: (sources[i], 0, 0))],
            out_specs=pl.BlockSpec((1, ROWS, FF), lambda i, sources: (i, 0, 0)),
        ),
        out_shape=jax.ShapeDtypeStruct((LOCAL, ROWS, FF), jnp.bfloat16),
        name="place",
    )(sources, returned)


def muon_kernel(
    outgoing,
    result,
    by_source,
    rows,
    squares,
    part,
    send_sum,
    recv_sum,
    strips,
    gram,
    normal,
    product,
    done,
    y_send,
    y_recv,
    x_send,
    x_recv,
    twin_send,
    twin_recv,
    sq_send,
    sq_recv,
    sum_send,
    sum_recv,
    all_send,
    all_recv,
    all_twin_send,
    all_twin_recv,
    back_send,
    back_recv,
):
    dp = lax.axis_index("dp")
    y = lax.axis_index("expert")
    x, z, core = dp // 16, (dp // 2) % RING, dp % 2

    def device(to_x, to_y, to_z, to_core):
        return (to_x * 16 + to_z * 2 + to_core, to_y)

    def turn(value, by, size):
        return lax.rem(value + (by % size), size)

    def remote(source, target, send, recv, where):
        return pltpu.make_async_remote_copy(
            src_ref=source,
            dst_ref=target,
            send_sem=send,
            recv_sem=recv,
            device_id=where,
            device_id_type=MESH,
        )

    def arrived(ref, sem):
        pltpu.make_async_copy(ref, ref, sem).wait()

    along_x = [turn(x, e, LOCAL) for e in range(LOCAL)]
    along_y = [turn(y, e, LOCAL) for e in range(LOCAL)]
    twin = device(x, y, z, 1 - core)

    barrier = pltpu.get_barrier_semaphore()
    partners = (
        [device(to, y, z, core) for to in along_x[1:]]
        + [device(x, to, z, core) for to in along_y[1:]]
        + [device(x, y, turn(z, e, RING), core) for e in range(1, RING)]
        + [twin]
    )
    for partner in partners:
        pl.semaphore_signal(barrier, inc=1, device_id=partner, device_id_type=MESH)
    pl.semaphore_wait(barrier, len(partners))

    pending = []

    chunks = [turn(z, 4 + t, RING) for t in range(RING)]
    for t, q in enumerate(chunks):
        for to in along_y[1:]:
            copy = remote(
                outgoing.at[q, to],
                by_source.at[q, y],
                y_send.at[t, to],
                y_recv.at[t, y],
                device(x, to, z, core),
            )
            copy.start()
            pending.append(copy)
        pltpu.make_async_copy(outgoing.at[q, y], by_source.at[q, y], y_recv.at[t, y]).start()

    def pass_on(t):
        q = chunks[t]
        for to in along_x[1:]:
            arrived(by_source.at[q, to], y_recv.at[t, to])
            copy = remote(
                by_source.at[q, to],
                rows.at[q, core, pl.ds(pl.multiple_of(x * ROWS, 16), ROWS)],
                x_send.at[t, to],
                x_recv.at[t, x],
                device(to, y, z, core),
            )
            copy.start()
            pending.append(copy)
        arrived(by_source.at[q, x], y_recv.at[t, x])
        pltpu.make_async_copy(
            by_source.at[q, x],
            rows.at[q, core, pl.ds(pl.multiple_of(x * ROWS, 16), ROWS)],
            x_recv.at[t, x],
        ).start()

    def share(t):
        q = chunks[t]
        for source in range(LOCAL):
            arrived(rows.at[q, core, pl.ds(source * ROWS, ROWS)], x_recv.at[t, source])
        copy = remote(
            rows.at[q, core], rows.at[q, core], twin_send.at[t], twin_recv.at[t], twin
        )
        copy.start()
        pending.append(copy)

    def shared(t):
        arrived(rows.at[chunks[t], 1 - core], twin_recv.at[t])

    lane = pl.multiple_of(core * HALF, HALF)

    def make_strip(k):
        left = rows[k, :, :, pl.ds(lane, HALF)].reshape(2 * OWNED, HALF)
        for f in range(LOCAL):
            right = rows[lax.rem(k + core + f, RING)].reshape(2 * OWNED, CHUNK)
            part[k, :, f * CHUNK : (f + 1) * CHUNK] = lax.dot_general(
                left, right, (((0,), (0,)), ((), ())), preferred_element_type=jnp.float32
            )
        last = lax.rem(k + 4 * (1 - core), RING)
        right = rows[last, :, :, pl.ds(lane, HALF)].reshape(2 * OWNED, HALF)
        part[k, :, WIDE:] = lax.dot_general(
            left, right, (((0,), (0,)), ((), ())), preferred_element_type=jnp.float32
        )

    ways = (1, -1)
    halves = (slice(PART, HALF), slice(0, PART))

    def pieces(way, only):
        return (halves[way],) if only else (halves[way], halves[1 - way])

    def piece_id(piece):
        return 0 if piece.start == 0 else 1

    def send_step(way, t):
        k = turn(z, ways[way] * (4 - t), RING)
        for piece in pieces(way, t == 0):
            h = piece_id(piece)
            value = part[k, piece]
            if t >= 2 or (t == 1 and piece == halves[way]):
                arrived(recv_sum.at[way, t - 1, piece], sum_recv.at[way, t - 1, h])
                value = value + recv_sum[way, t - 1, piece].astype(jnp.float32)
            send_sum[way, t, piece] = value.astype(jnp.bfloat16)
            copy = remote(
                send_sum.at[way, t, piece],
                recv_sum.at[way, t, piece],
                sum_send.at[way, t, h],
                sum_recv.at[way, t, h],
                device(x, y, turn(z, ways[way], RING), core),
            )
            copy.start()
            pending.append(copy)

    for t in range(RING + 2):
        if t < RING:
            pass_on(t)
        if 1 <= t <= RING:
            share(t - 1)
        if t >= 2:
            shared(t - 2)
            if t - 2 == 4:
                make_strip(turn(z, 4, RING))
                send_step(0, 0)
                send_step(1, 0)
            if t - 2 == 5:
                make_strip(turn(z, -3, RING))
            if t - 2 == 6:
                make_strip(turn(z, -2, RING))
                send_step(1, 1)
    make_strip(turn(z, 3, RING))
    send_step(0, 1)

    total = jnp.zeros((1, CHUNK), jnp.float32)
    for q in range(RING):
        values = rows[q].reshape(2 * OWNED, CHUNK).astype(jnp.float32)
        total = total + jnp.sum(values * values, axis=0, keepdims=True)
    squares[z] = jnp.broadcast_to(total[:, :HALF] + total[:, HALF:], (8, HALF))
    for e in range(1, RING):
        copy = remote(
            squares.at[z],
            squares.at[z],
            sq_send.at[e],
            sq_recv.at[e],
            device(x, y, turn(z, e, RING), core),
        )
        copy.start()
        pending.append(copy)

    make_strip(turn(z, 2, RING))
    send_step(1, 2)
    send_step(0, 2)
    make_strip(turn(z, -1, RING))
    make_strip(turn(z, 1, RING))
    send_step(1, 3)
    send_step(0, 3)
    make_strip(z)

    for e in range(1, RING):
        arrived(squares.at[turn(z, -e, RING)], sq_recv.at[e])
    everything = jnp.sum(
        jnp.sum(squares[:, 0, :], axis=0, keepdims=True), axis=1, keepdims=True
    )
    factor = 0.5 * math.sqrt(FF) / jnp.sqrt(everything + 1e-6)
    for q in range(RING):
        normal[:, q * CHUNK : (q + 1) * CHUNK] = (
            rows[q, core].astype(jnp.float32) * factor
        ).astype(jnp.bfloat16)

    def spread_step(way, t):
        k = turn(z, -ways[way] * t, RING)
        for piece in pieces(way, t == 3):
            h = piece_id(piece)
            if t > 0:
                arrived(strips.at[core, k, piece], all_recv.at[way, t - 1, h])
            copy = remote(
                strips.at[core, k, piece],
                strips.at[core, k, piece],
                all_send.at[way, t, h],
                all_recv.at[way, t, h],
                device(x, y, turn(z, ways[way], RING), core),
            )
            copy.start()
            pending.append(copy)
        if t == 3:
            piece = halves[1 - way]
            arrived(strips.at[core, k, piece], all_recv.at[way, t - 1, piece_id(piece)])

    def give_twin(k, n):
        copy = remote(
            strips.at[core, k],
            strips.at[core, k],
            all_twin_send.at[n],
            all_twin_recv.at[n],
            twin,
        )
        copy.start()
        pending.append(copy)

    def lay(which, k):
        at = pl.multiple_of(k * CHUNK + which * HALF, HALF)
        for f in range(LOCAL):
            q = lax.rem(k + which + f, RING)
            block = strips[which, k, :, f * CHUNK : (f + 1) * CHUNK]
            to = pl.multiple_of(q * CHUNK, CHUNK)
            gram[pl.ds(at, HALF), pl.ds(to, CHUNK)] = block
            gram[pl.ds(to, CHUNK), pl.ds(at, HALF)] = block.T
        q = lax.rem(k + 4 * (1 - which), RING)
        to = pl.multiple_of(q * CHUNK + which * HALF, HALF)
        gram[pl.ds(at, HALF), pl.ds(to, HALF)] = strips[which, k, :, WIDE:]

    scale = factor * factor
    for way in range(2):
        for piece in halves:
            arrived(recv_sum.at[way, 3, piece], sum_recv.at[way, 3, piece_id(piece)])
    strips[core, z] = (
        (
            part[z]
            + recv_sum[0, 3].astype(jnp.float32)
            + recv_sum[1, 3].astype(jnp.float32)
        )
        * scale
    ).astype(jnp.bfloat16)

    names = [z]
    for t in range(4):
        spread_step(0, t)
        spread_step(1, t)
        if t == 0:
            give_twin(z, 0)
            lay(core, z)
        else:
            below, above = turn(z, -t, RING), turn(z, t, RING)
            give_twin(below, 2 * t - 1)
            give_twin(above, 2 * t)
            names += [below, above]
            lay(core, below)
            lay(core, above)
            for n in (2 * t - 3, 2 * t - 2) if t > 1 else (0,):
                arrived(strips.at[1 - core, names[n]], all_twin_recv.at[n])
                lay(1 - core, names[n])
    for n in (5, 6):
        arrived(strips.at[1 - core, names[n]], all_twin_recv.at[n])
        lay(1 - core, names[n])
    far = turn(z, 4, RING)
    for way in range(2):
        arrived(strips.at[core, far, halves[way]], all_recv.at[way, 3, piece_id(halves[way])])
    give_twin(far, 7)
    lay(core, far)
    arrived(strips.at[1 - core, far], all_twin_recv.at[7])
    lay(1 - core, far)

    def first(q, carry):
        at = pl.ds(pl.multiple_of(q * CHUNK, CHUNK), CHUNK)
        product[:, at] = jnp.dot(
            normal[...], gram[:, at], preferred_element_type=jnp.float32
        ).astype(jnp.bfloat16)
        return carry

    lax.fori_loop(0, RING, first, 0)

    for q in range(RING):
        at = slice(q * CHUNK, (q + 1) * CHUNK)
        second = jnp.dot(product[...], gram[:, at], preferred_element_type=jnp.float32)
        orthogonal = (
            3.4445 * normal[:, at].astype(jnp.float32)
            - 4.775 * product[:, at].astype(jnp.float32)
            + 2.0315 * second
        )
        done[q] = (orthogonal * math.sqrt(D)).astype(jnp.bfloat16)
        for to in along_x[1:]:
            copy = remote(
                done.at[q, pl.ds(pl.multiple_of(to * ROWS, 16), ROWS)],
                result.at[x, :, at],
                back_send.at[q, to],
                back_recv.at[q, x],
                device(to, y, z, core),
            )
            copy.start()
            pending.append(copy)
        pltpu.make_async_copy(
            done.at[q, pl.ds(pl.multiple_of(x * ROWS, 16), ROWS)],
            result.at[x, :, at],
            back_recv.at[q, x],
        ).start()
    for q in range(RING):
        for source in range(LOCAL):
            arrived(result.at[source, :, q * CHUNK : (q + 1) * CHUNK], back_recv.at[q, source])
    for copy in pending:
        copy.wait_send()


def muon(outgoing):
    dma = pltpu.SemaphoreType.DMA
    bf16, f32 = jnp.bfloat16, jnp.float32
    return pl.pallas_call(
        muon_kernel,
        out_shape=jax.ShapeDtypeStruct((LOCAL, ROWS, FF), bf16),
        in_specs=[pl.BlockSpec(memory_space=pltpu.VMEM)],
        out_specs=pl.BlockSpec(memory_space=pl.ANY),
        scratch_shapes=[
            pltpu.VMEM((RING, LOCAL, ROWS, CHUNK), bf16),
            pltpu.VMEM((RING, 2, OWNED, CHUNK), bf16),
            pltpu.VMEM((RING, 8, 128), f32),
            pltpu.VMEM((RING, HALF, STRIP), f32),
            pltpu.VMEM((2, 4, HALF, STRIP), bf16),
            pltpu.VMEM((2, 4, HALF, STRIP), bf16),
            pltpu.VMEM((2, RING, HALF, STRIP), bf16),
            pltpu.VMEM((FF, FF), bf16),
            pltpu.VMEM((OWNED, FF), bf16),
            pltpu.VMEM((OWNED, FF), bf16),
            pltpu.VMEM((RING, OWNED, CHUNK), bf16),
            dma((RING, LOCAL)),
            dma((RING, LOCAL)),
            dma((RING, LOCAL)),
            dma((RING, LOCAL)),
            dma((RING,)),
            dma((RING,)),
            dma((RING,)),
            dma((RING,)),
            dma((2, 4, 2)),
            dma((2, 4, 2)),
            dma((2, 4, 2)),
            dma((2, 4, 2)),
            dma((RING,)),
            dma((RING,)),
            dma((RING, LOCAL)),
            dma((RING, LOCAL)),
        ],
        compiler_params=pltpu.CompilerParams(
            collective_id=0, has_side_effects=True, vmem_limit_bytes=56 << 20
        ),
        name="muon",
    )(outgoing)


def shards(grad, momentum, placement):
    group = lax.axis_index("expert")
    ids = lax.iota(jnp.int32, LOCAL)
    targets = lax.dynamic_slice_in_dim(placement, group * LOCAL, LOCAL) // LOCAL
    send_slots = jnp.sum((targets[None, :] == ids[:, None]) * ids[None, :], axis=1)
    table = placement.reshape(LOCAL, LOCAL)
    new_slot = jnp.sum(jnp.where(table // LOCAL == group, table % LOCAL, 0), axis=1)
    sources = jnp.sum((new_slot[None, :] == ids[:, None]) * ids[None, :], axis=1)
    momentum_new, outgoing = prepare(send_slots.astype(jnp.int32), grad, momentum)
    update = place(sources.astype(jnp.int32), muon(outgoing))
    return (momentum_new, update)


def solution(mesh):
    return jax.shard_map(
        shards,
        mesh=mesh,
        in_specs=(P("expert", "dp", None), P("expert", "dp", None), P()),
        out_specs=(P("expert", "dp", None), P("expert", "dp", None)),
        check_vma=False,
    )
```

time: 744 us -> 140 us (0.19)
  waiting for transfers between devices: 438 us -> 0 us
  blocking collectives: 180 us -> 0 us
  Pallas kernels: 0 us -> 132 us
  other arithmetic: 53.7 us -> 1.62 us
  matrix products: 25.9 us -> 0 us
  starting transfers between devices: 25.7 us -> 0 us
  local copies, waits for them, and re-layouts: 19.1 us -> 5.5 us
    ppermute x8 -> x0, waiting for transfers between devices: 365 us -> none  [from_partner(): return lax.ppermute(value, axis, pairs)]
    pallas_call x0 -> x3, Pallas kernels: none -> 132 us  [the longest x1 123 us: muon(): pl.pallas_call(muon_kernel, out_shape=jax.ShapeDtypeStruct((LOCAL, ROWS,...]
    psum x1 -> x0, blocking collectives: 124 us -> none  [shards(): totals = lax.psum(partial_value * in_block, 'dp')]
    all_to_all x2 -> x0, waiting for transfers between devices: 72.6 us -> none  [the longest x1 51.2 us: shards(): lax.all_to_all(outgoing_rows, 'dp', split_axis=0, concat_axis=0, tiled=True)]
    all_to_all x1 -> x0, blocking collectives: 56.1 us -> none  [shards(): lax.all_to_all(result.reshape(dp_count, piece_rows, columns), 'dp', split...]
    dot_general x3 -> x0, matrix products: 25.9 us -> none  [the longest x1 9.27 us: shards(): second = jnp.dot(product, gram_whole, preferred_element_type=jnp.float32)]
    select_n x12 -> x1, other arithmetic: 24.1 us -> 0.74 us  [shards(): targets = lax.dynamic_slice_in_dim(placement, group * LOCAL, LOCAL) // LOCAL]
    all_to_all x2 -> x0, starting transfers between devices: 19.2 us -> none  [the longest x1 14.2 us: shards(): lax.all_to_all(outgoing_rows, 'dp', split_axis=0, concat_axis=0, tiled=True)]
  transfers between devices with their start and end apart: 10 -> 0, of which waited for: 10 -> 0; matrix products, arithmetic and copies ran while one was open for 0% -> 0% of each run, Pallas kernels for 0% -> 0%
where the time goes in v1:
time: 140 us
  Pallas kernels  132 us (94%)
  local copies, waits for them, and re-layouts  5.5 us (4%)
  other arithmetic  1.62 us (1%)
    pallas_call x1, Pallas kernels, muon(): pl.pallas_call(muon_kernel, out_shape=jax.ShapeDtypeStruct((LOCAL, ROWS,...  123 us
    unnamed x6, local copies, waits for them, and re-layouts  4.76 us
    pallas_call x1, Pallas kernels, place(): pl.pallas_call(place_kernel, grid_spec=pltpu.PrefetchScalarGridSpec(num_s...  4.34 us
    pallas_call x1, Pallas kernels, prepare(): pl.pallas_call(prep_kernel, grid_spec=pltpu.PrefetchScalarGridSpec(num_sc...  4.31 us

profile of v1, /device:TPU:1, one launch (start us, length us, event | category | flops | bytes accessed | tf_op | source)
XLA Modules:
  0.0 139.9 jit_solution(3887751167099472259)
XLA Ops:
  0.6 0.7 and_select_fusion
  1.4 0.1 select_reduce_fusion.1.slots_ref
  1.5 0.7 reshape.9
  2.2 0.1 fusion.2
  2.4 0.6 select_reduce_fusion.sources_ref
  3.0 0.0 copy-start
  3.0 2.0 %copy-done = f32[4,112,2048]{2,1,0:T(8,128)S(1)} copy-done((f32[4,112,2048]{2,1,0:T(8,128)S(1)}, f32[4,112,2048]{2,1,0:T(8,128)}, u32[]{:S(2)}) %copy-start) | copy-done | bytes 3670040
  5.0 0.0 copy-start.2
  5.0 1.5 %copy-done.2 = bf16[4,112,2048]{2,1,0:T(8,128)(2,1)S(1)} copy-done((bf16[4,112,2048]{2,1,0:T(8,128)(2,1)S(1)}, bf16[4,112,2048]{2,1,0:T(8,128)(2,1)}, u32[]{:S(2)}) %copy-start.2) | copy-done | bytes 1835032
  6.5 4.3 %prepare.1 = (f32[4,112,2048]{2,1,0:T(8,128)}, bf16[8,4,112,256]{3,2,1,0:T(8,128)(2,1)S(1)}) custom-call(s32[4]{0:T(128)S(1)} %select_reduce_fusion.1.slots_ref, bf16[4,112,2048]{2,1,0:T(8,128)(2,1)S(1)} %copy-done.2, f32[4,112,2048]{2,1,0:T(8,128)S(1)} %copy-done), custom_call_target="tpu_custom_call" | custom-call | tf_op jit(solution)/shard_map/prepare/pallas_call | solution.py:37
  10.8 0.0 copy-start.1
  10.9 1.2 copy-done.1
  12.1 123.5 %muon.1.from_ref = bf16[4,112,2048]{2,1,0:T(8,128)(2,1)} custom-call(bf16[8,4,112,256]{3,2,1,0:T(8,128)(2,1)} %copy-done.1), custom_call_target="tpu_custom_call" | custom-call | tf_op jit(solution)/shard_map/muon/pallas_call | solution.py:417
  135.6 4.3 %place.1 = bf16[4,112,2048]{2,1,0:T(8,128)(2,1)} custom-call(s32[4]{0:T(128)} %select_reduce_fusion.sources_ref, bf16[4,112,2048]{2,1,0:T(8,128)(2,1)} %muon.1.from_ref), custom_call_target="tpu_custom_call" | custom-call | tf_op jit(solution)/shard_map/place/pallas_call | solution.py:62
Async XLA Ops:
  3.0 2.0 %copy-start = (f32[4,112,2048]{2,1,0:T(8,128)S(1)}, f32[4,112,2048]{2,1,0:T(8,128)}, u32[]{:S(2)}) copy-start(f32[4,112,2048]{2,1,0:T(8,128)} %momentum_ref.1) | copy-start | bytes 11010052
  5.0 1.5 %copy-start.2 = (bf16[4,112,2048]{2,1,0:T(8,128)(2,1)S(1)}, bf16[4,112,2048]{2,1,0:T(8,128)(2,1)}, u32[]{:S(2)}) copy-start(bf16[4,112,2048]{2,1,0:T(8,128)(2,1)} %grad_ref.1) | copy-start | bytes 5505028
  10.8 1.2 copy-start.1

commit v2 on v1

v2 whole, which is shorter than its diff:
```python
import functools
import math

import jax
import jax.numpy as jnp
from jax import lax
from jax.experimental import pallas as pl
from jax.experimental.pallas import tpu as pltpu
from jax.sharding import PartitionSpec as P

D = 7168
MESH = pl.DeviceIdType.MESH
LOCAL = 4
RING = 8
ROWS = 112
OWNED = LOCAL * ROWS
FF = 2048
CHUNK = FF // RING
HALF = CHUNK // 2
WIDE = LOCAL * CHUNK
STRIP = WIDE + HALF
PIECES = 4
PART = HALF // PIECES


def muon_kernel(
    placement,
    grad,
    momentum,
    update,
    grad_in,
    momentum_in,
    outgoing,
    returned,
    placed,
    by_source,
    rows,
    squares,
    part,
    send_sum,
    recv_sum,
    strips,
    gram,
    normal,
    product,
    done,
    load_sem,
    store_sem,
    y_send,
    y_recv,
    x_send,
    x_recv,
    twin_send,
    twin_recv,
    sq_send,
    sq_recv,
    sum_send,
    sum_recv,
    all_send,
    all_recv,
    all_twin_send,
    all_twin_recv,
    back_send,
    back_recv,
):
    dp = lax.axis_index("dp")
    y = lax.axis_index("expert")
    x, z, core = dp // 16, (dp // 2) % RING, dp % 2

    def device(to_x, to_y, to_z, to_core):
        return (to_x * 16 + to_z * 2 + to_core, to_y)

    def turn(value, by, size):
        return lax.rem(value + (by % size), size)

    def remote(source, target, send, recv, where):
        return pltpu.make_async_remote_copy(
            src_ref=source,
            dst_ref=target,
            send_sem=send,
            recv_sem=recv,
            device_id=where,
            device_id_type=MESH,
        )

    def arrived(ref, sem):
        pltpu.make_async_copy(ref, ref, sem).wait()

    chunks = [turn(z, 4 + t, RING) for t in range(RING)]

    def columns(q):
        return pl.ds(pl.multiple_of(q * CHUNK, CHUNK), CHUNK)

    loads = []
    for t, q in enumerate(chunks):
        pair = [
            pltpu.make_async_copy(grad.at[:, :, columns(q)], grad_in[t], load_sem.at[t, 0]),
            pltpu.make_async_copy(
                momentum.at[:, :, columns(q)], momentum_in[t], load_sem.at[t, 1]
            ),
        ]
        for copy in pair:
            copy.start()
        loads.append(pair)

    chosen, origin = [], []
    for place in range(LOCAL):
        slot, source = jnp.int32(0), jnp.int32(0)
        for j in range(1, LOCAL):
            goes = placement[y * LOCAL + j] // LOCAL
            slot = jnp.where(goes == place, j, slot)
        for e in range(LOCAL, LOCAL * LOCAL):
            source = jnp.where(placement[e] == y * LOCAL + place, e // LOCAL, source)
        chosen.append(slot)
        origin.append(source)

    along_x = [turn(x, e, LOCAL) for e in range(LOCAL)]
    along_y = [turn(y, e, LOCAL) for e in range(LOCAL)]
    twin = device(x, y, z, 1 - core)

    barrier = pltpu.get_barrier_semaphore()
    partners = (
        [device(to, y, z, core) for to in along_x[1:]]
        + [device(x, to, z, core) for to in along_y[1:]]
        + [device(x, y, turn(z, e, RING), core) for e in range(1, RING)]
        + [twin]
    )
    for partner in partners:
        pl.semaphore_signal(barrier, inc=1, device_id=partner, device_id_type=MESH)
    pl.semaphore_wait(barrier, len(partners))

    pending = []

    def depart(t):
        for copy in loads[t]:
            copy.wait()
        q = chunks[t]
        for to in range(LOCAL):
            new = 0.95 * momentum_in[t][chosen[to]] + grad_in[t][chosen[to]].astype(jnp.float32)
            outgoing[q, to] = new.astype(jnp.bfloat16)
        sent = []
        for to in along_y[1:]:
            copy = remote(
                outgoing.at[q, to],
                by_source.at[q, y],
                y_send.at[t, to],
                y_recv.at[t, y],
                device(x, to, z, core),
            )
            copy.start()
            sent.append(copy)
        pltpu.make_async_copy(outgoing.at[q, y], by_source.at[q, y], y_recv.at[t, y]).start()
        return sent

    def pass_on(t):
        q = chunks[t]
        for to in along_x[1:]:
            arrived(by_source.at[q, to], y_recv.at[t, to])
            copy = remote(
                by_source.at[q, to],
                rows.at[q, core, pl.ds(pl.multiple_of(x * ROWS, 16), ROWS)],
                x_send.at[t, to],
                x_recv.at[t, x],
                device(to, y, z, core),
            )
            copy.start()
            pending.append(copy)
        arrived(by_source.at[q, x], y_recv.at[t, x])
        pltpu.make_async_copy(
            by_source.at[q, x],
            rows.at[q, core, pl.ds(pl.multiple_of(x * ROWS, 16), ROWS)],
            x_recv.at[t, x],
        ).start()

    def share(t):
        q = chunks[t]
        for source in range(LOCAL):
            arrived(rows.at[q, core, pl.ds(source * ROWS, ROWS)], x_recv.at[t, source])
        copy = remote(
            rows.at[q, core], rows.at[q, core], twin_send.at[t], twin_recv.at[t], twin
        )
        copy.start()
        pending.append(copy)

    def shared(t):
        arrived(rows.at[chunks[t], 1 - core], twin_recv.at[t])

    lane = pl.multiple_of(core * HALF, HALF)

    def make_strip(k):
        left = rows[k, :, :, pl.ds(lane, HALF)].reshape(2 * OWNED, HALF)
        for f in range(LOCAL):
            right = rows[lax.rem(k + core + f, RING)].reshape(2 * OWNED, CHUNK)
            part[k, :, f * CHUNK : (f + 1) * CHUNK] = lax.dot_general(
                left, right, (((0,), (0,)), ((), ())), preferred_element_type=jnp.float32
            )
        last = lax.rem(k + 4 * (1 - core), RING)
        right = rows[last, :, :, pl.ds(lane, HALF)].reshape(2 * OWNED, HALF)
        part[k, :, WIDE:] = lax.dot_general(
            left, right, (((0,), (0,)), ((), ())), preferred_element_type=jnp.float32
        )

    ways = (1, -1)
    rows_of = [slice(n * PART, (n + 1) * PART) for n in range(PIECES)]
    half = PIECES // 2
    order = (tuple(range(half, PIECES)) + tuple(range(half)), tuple(range(PIECES)))

    def from_far(way):
        return order[way][:half]

    def send_piece(way, t, n):
        k = turn(z, ways[way] * (4 - t), RING)
        piece = rows_of[n]
        value = part[k, piece]
        if t >= 2 or (t == 1 and n in from_far(way)):
            arrived(recv_sum.at[way, t - 1, piece], sum_recv.at[way, t - 1, n])
            value = value + recv_sum[way, t - 1, piece].astype(jnp.float32)
        send_sum[way, t, piece] = value.astype(jnp.bfloat16)
        copy = remote(
            send_sum.at[way, t, piece],
            recv_sum.at[way, t, piece],
            sum_send.at[way, t, n],
            sum_recv.at[way, t, n],
            device(x, y, turn(z, ways[way], RING), core),
        )
        copy.start()
        pending.append(copy)

    def send_step(t, which=(0, 1)):
        for i in range(PIECES if t else half):
            for way in which:
                send_piece(way, t, order[way][i])

    in_flight = [depart(0), depart(1)]
    for t in range(RING + 2):
        if t < RING:
            pass_on(t)
            for copy in in_flight[t]:
                copy.wait_send()
            if t + 2 < RING:
                in_flight.append(depart(t + 2))
        if 1 <= t <= RING:
            share(t - 1)
        if t >= 2:
            shared(t - 2)
            if t - 2 == 4:
                make_strip(turn(z, 4, RING))
                send_step(0)
            if t - 2 == 5:
                make_strip(turn(z, -3, RING))
            if t - 2 == 6:
                make_strip(turn(z, -2, RING))
                send_step(1, (1,))
    make_strip(turn(z, 3, RING))
    send_step(1, (0,))

    total = jnp.zeros((1, CHUNK), jnp.float32)
    for q in range(RING):
        values = rows[q].reshape(2 * OWNED, CHUNK).astype(jnp.float32)
        total = total + jnp.sum(values * values, axis=0, keepdims=True)
    squares[z] = jnp.broadcast_to(total[:, :HALF] + total[:, HALF:], (8, HALF))
    for e in range(1, RING):
        copy = remote(
            squares.at[z],
            squares.at[z],
            sq_send.at[e],
            sq_recv.at[e],
            device(x, y, turn(z, e, RING), core),
        )
        copy.start()
        pending.append(copy)

    make_strip(turn(z, 2, RING))
    send_step(2)
    make_strip(turn(z, -1, RING))
    make_strip(turn(z, 1, RING))
    send_step(3)
    make_strip(z)

    for e in range(1, RING):
        arrived(squares.at[turn(z, -e, RING)], sq_recv.at[e])
    everything = jnp.sum(
        jnp.sum(squares[:, 0, :], axis=0, keepdims=True), axis=1, keepdims=True
    )
    factor = 0.5 * math.sqrt(FF) / jnp.sqrt(everything + 1e-6)
    for q in range(RING):
        normal[:, q * CHUNK : (q + 1) * CHUNK] = (
            rows[q, core].astype(jnp.float32) * factor
        ).astype(jnp.bfloat16)

    def spread_piece(way, t, n):
        k = turn(z, -ways[way] * t, RING)
        piece = rows_of[n]
        if t > 0:
            arrived(strips.at[core, k, piece], all_recv.at[way, t - 1, n])
        if t == 3 and n not in from_far(way):
            return None
        copy = remote(
            strips.at[core, k, piece],
            strips.at[core, k, piece],
            all_send.at[way, t, n],
            all_recv.at[way, t, n],
            device(x, y, turn(z, ways[way], RING), core),
        )
        copy.start()
        return copy

    def give_twin(k, n):
        copy = remote(
            strips.at[core, k],
            strips.at[core, k],
            all_twin_send.at[n],
            all_twin_recv.at[n],
            twin,
        )
        copy.start()
        pending.append(copy)

    def lay(which, k):
        at = pl.multiple_of(k * CHUNK + which * HALF, HALF)
        for f in range(LOCAL):
            q = lax.rem(k + which + f, RING)
            block = strips[which, k, :, f * CHUNK : (f + 1) * CHUNK]
            to = pl.multiple_of(q * CHUNK, CHUNK)
            gram[pl.ds(at, HALF), pl.ds(to, CHUNK)] = block
            gram[pl.ds(to, CHUNK), pl.ds(at, HALF)] = block.T
        q = lax.rem(k + 4 * (1 - which), RING)
        to = pl.multiple_of(q * CHUNK + which * HALF, HALF)
        gram[pl.ds(at, HALF), pl.ds(to, HALF)] = strips[which, k, :, WIDE:]

    scale = factor * factor
    sent = []
    for n in range(PIECES):
        piece = rows_of[n]
        for way in range(2):
            arrived(recv_sum.at[way, 3, piece], sum_recv.at[way, 3, n])
        strips[core, z, piece] = (
            (
                part[z, piece]
                + recv_sum[0, 3, piece].astype(jnp.float32)
                + recv_sum[1, 3, piece].astype(jnp.float32)
            )
            * scale
        ).astype(jnp.bfloat16)
        for way in range(2):
            sent.append(spread_piece(way, 0, n))
    give_twin(z, 0)
    lay(core, z)
    pending.extend(sent)

    def lay_twin(k, n):
        arrived(strips.at[1 - core, k], all_twin_recv.at[n])
        lay(1 - core, k)

    tasks = [lambda: lay_twin(z, 0)]
    for t in range(1, 4):
        for i in range(PIECES):
            for way in range(2):
                copy = spread_piece(way, t, order[way][i])
                if copy is not None:
                    pending.append(copy)
            if tasks:
                tasks.pop(0)()
        below, above = turn(z, -t, RING), turn(z, t, RING)
        give_twin(below, 2 * t - 1)
        give_twin(above, 2 * t)
        tasks += [
            functools.partial(lay, core, below),
            functools.partial(lay, core, above),
            functools.partial(lay_twin, below, 2 * t - 1),
            functools.partial(lay_twin, above, 2 * t),
        ]
    for task in tasks:
        task()
    far = turn(z, 4, RING)
    for way in range(2):
        for n in from_far(way):
            arrived(strips.at[core, far, rows_of[n]], all_recv.at[way, 3, n])
    give_twin(far, 7)
    lay(core, far)
    lay_twin(far, 7)

    def first(q, carry):
        at = pl.ds(pl.multiple_of(q * CHUNK, CHUNK), CHUNK)
        product[:, at] = jnp.dot(
            normal[...], gram[:, at], preferred_element_type=jnp.float32
        ).astype(jnp.bfloat16)
        return carry

    lax.fori_loop(0, RING, first, 0)

    for q in range(RING):
        at = slice(q * CHUNK, (q + 1) * CHUNK)
        second = jnp.dot(product[...], gram[:, at], preferred_element_type=jnp.float32)
        orthogonal = (
            3.4445 * normal[:, at].astype(jnp.float32)
            - 4.775 * product[:, at].astype(jnp.float32)
            + 2.0315 * second
        )
        done[q] = (orthogonal * math.sqrt(D)).astype(jnp.bfloat16)
        for to in along_x[1:]:
            copy = remote(
                done.at[q, pl.ds(pl.multiple_of(to * ROWS, 16), ROWS)],
                returned[q].at[x],
                back_send.at[q, to],
                back_recv.at[q, x],
                device(to, y, z, core),
            )
            copy.start()
            pending.append(copy)
        pltpu.make_async_copy(
            done.at[q, pl.ds(pl.multiple_of(x * ROWS, 16), ROWS)],
            returned[q].at[x],
            back_recv.at[q, x],
        ).start()
    stores = []
    for q in range(RING):
        at = slice(q * CHUNK, (q + 1) * CHUNK)
        for source in range(LOCAL):
            arrived(returned[q].at[source], back_recv.at[q, source])
        for place in range(LOCAL):
            placed[place, :, at] = returned[q][origin[place]]
        copy = pltpu.make_async_copy(placed.at[:, :, at], update.at[:, :, at], store_sem.at[q])
        copy.start()
        stores.append(copy)
    for copy in stores:
        copy.wait()
    for copy in pending:
        copy.wait_send()


def muon(placement, grad, momentum):
    dma = pltpu.SemaphoreType.DMA
    bf16, f32 = jnp.bfloat16, jnp.float32
    return pl.pallas_call(
        muon_kernel,
        out_shape=jax.ShapeDtypeStruct((LOCAL, ROWS, FF), bf16),
        in_specs=[
            pl.BlockSpec(memory_space=pltpu.SMEM),
            pl.BlockSpec(memory_space=pl.ANY),
            pl.BlockSpec(memory_space=pl.ANY),
        ],
        out_specs=pl.BlockSpec(memory_space=pl.ANY),
        scratch_shapes=[
            [pltpu.VMEM((LOCAL, ROWS, CHUNK), bf16)] * RING,
            [pltpu.VMEM((LOCAL, ROWS, CHUNK), f32)] * RING,
            pltpu.VMEM((RING, LOCAL, ROWS, CHUNK), bf16),
            [pltpu.VMEM((LOCAL, ROWS, CHUNK), bf16)] * RING,
            pltpu.VMEM((LOCAL, ROWS, FF), bf16),
            pltpu.VMEM((RING, LOCAL, ROWS, CHUNK), bf16),
            pltpu.VMEM((RING, 2, OWNED, CHUNK), bf16),
            pltpu.VMEM((RING, 8, 128), f32),
            pltpu.VMEM((RING, HALF, STRIP), f32),
            pltpu.VMEM((2, 4, HALF, STRIP), bf16),
            pltpu.VMEM((2, 4, HALF, STRIP), bf16),
            pltpu.VMEM((2, RING, HALF, STRIP), bf16),
            pltpu.VMEM((FF, FF), bf16),
            pltpu.VMEM((OWNED, FF), bf16),
            pltpu.VMEM((OWNED, FF), bf16),
            pltpu.VMEM((RING, OWNED, CHUNK), bf16),
            dma((RING, 2)),
            dma((RING,)),
            dma((RING, LOCAL)),
            dma((RING, LOCAL)),
            dma((RING, LOCAL)),
            dma((RING, LOCAL)),
            dma((RING,)),
            dma((RING,)),
            dma((RING,)),
            dma((RING,)),
            dma((2, 4, PIECES)),
            dma((2, 4, PIECES)),
            dma((2, 4, PIECES)),
            dma((2, 4, PIECES)),
            dma((RING,)),
            dma((RING,)),
            dma((RING, LOCAL)),
            dma((RING, LOCAL)),
        ],
        compiler_params=pltpu.CompilerParams(
            collective_id=0, has_side_effects=True, vmem_limit_bytes=60 << 20
        ),
        name="muon",
    )(placement, grad, momentum)


def shards(grad, momentum, placement):
    update = muon(placement, grad, momentum)
    momentum_new = 0.95 * momentum + grad.astype(jnp.float32)
    return (momentum_new, update)


def solution(mesh):
    return jax.shard_map(
        shards,
        mesh=mesh,
        in_specs=(P("expert", "dp", None), P("expert", "dp", None), P()),
        out_specs=(P("expert", "dp", None), P("expert", "dp", None)),
        check_vma=False,
    )
```

time: 140 us -> 128 us (0.914)
  Pallas kernels: 132 us -> 122 us
  local copies, waits for them, and re-layouts: 5.5 us -> 1.24 us
  other arithmetic: 1.62 us -> 4.29 us
    pallas_call x2 -> x0, Pallas kernels: 8.66 us -> none  [the longest x1 4.34 us: place(): pl.pallas_call(place_kernel, grid_spec=pltpu.PrefetchScalarGridSpec(num_s...]
    add x0 -> x1, other arithmetic: none -> 4.29 us  [shards(): momentum_new = 0.95 * momentum + grad.astype(jnp.float32)]
    unnamed x6 -> x5, local copies, waits for them, and re-layouts: 4.76 us -> 1.24 us
    pallas_call x1, Pallas kernels: 123 us -> 122 us  [muon(): pl.pallas_call(muon_kernel, out_shape=jax.ShapeDtypeStruct((LOCAL, ROWS,...]
where the time goes in v2:
time: 128 us
  Pallas kernels  122 us (95%)
  other arithmetic  4.29 us (3%)
    pallas_call x1, Pallas kernels, muon(): pl.pallas_call(muon_kernel, out_shape=jax.ShapeDtypeStruct((LOCAL, ROWS,...  122 us
    add x1, other arithmetic, shards(): momentum_new = 0.95 * momentum + grad.astype(jnp.float32)  4.29 us

profile of v2, /device:TPU:1, one launch (start us, length us, event | category | flops | bytes accessed | tf_op | source)
XLA Modules:
  0.0 128.2 jit_solution(9446807198524597573)
XLA Ops:
  0.6 0.0 copy-start
  0.6 122.1 %muon.1 = bf16[4,112,2048]{2,1,0:T(8,128)(2,1)} custom-call(s32[16]{0:T(128)} %placement.1, bf16[4,112,2048]{2,1,0:T(8,128)(2,1)} %grad.1, f32[4,112,2048]{2,1,0:T(8,128)} %momentum.1), custom_call_target="tpu_custom_call" | custom-call | tf_op jit(solution)/shard_map/muon/pallas_call | solution.py:435
  122.7 0.0 copy-done
  122.7 0.0 copy-start.1
  122.7 4.3 %convert_add_fusion = f32[4,112,2048]{2,1,0:T(8,128)} fusion(bf16[4,112,2048]{2,1,0:T(8,128)(2,1)} %grad.1, f32[4,112,2048]{2,1,0:T(8,128)S(1)} %copy-done), kind=kLoop, calls=%fused_computation | loop fusion | flops 2752512 | bytes 9175040 | tf_op jit(solution)/shard_map/add | solution.py:489
  127.0 0.0 copy-done.1
  127.0 1.2 copy.6
Async XLA Ops:
  0.6 122.1 %copy-start = (f32[4,112,2048]{2,1,0:T(8,128)S(1)}, f32[4,112,2048]{2,1,0:T(8,128)}, u32[]{:S(2)}) copy-start(f32[4,112,2048]{2,1,0:T(8,128)} %momentum.1) | copy-start | bytes 11010052
  122.7 4.3 %copy-start.1 = (bf16[4,112,2048]{2,1,0:T(8,128)(2,1)S(1)}, bf16[4,112,2048]{2,1,0:T(8,128)(2,1)}, u32[]{:S(2)}) copy-start(bf16[4,112,2048]{2,1,0:T(8,128)(2,1)} %muon.1) | copy-start | bytes 5505028

commit v3 on v2

--- a/solution.py
+++ b/solution.py
@@ -19,8 +19,36 @@
 HALF = CHUNK // 2
 WIDE = LOCAL * CHUNK
 STRIP = WIDE + HALF
-PIECES = 4
-PART = HALF // PIECES
+PIECES = 5
+COLUMNS = tuple(slice(f * CHUNK, min((f + 1) * CHUNK, STRIP)) for f in range(PIECES))
+ORDER = (4, 5, 6, 3, 7, 2, 0, 1)
+FAR = ((0, 1), (2, 3, 4))
+
+
+def owner(way, step):
+    return (step - 4 if way else 4 - step) % RING
+
+
+def plan():
+    took, delay = (0.5, 0.5, 0.5, 0.5, 0.25), 0.9
+    events = []
+    for way in range(2):
+        todo = [(t, f) for t in range(4) for f in range(PIECES) if t or f in FAR[way]]
+        came, free = {}, 0.0
+        while todo:
+            options = []
+            for t, f in todo:
+                k = owner(way, t)
+                ready = 1.0 + max(ORDER.index(k), ORDER.index((k + f) % RING))
+                if t > 1 or (t == 1 and f in FAR[way]):
+                    ready = max(ready, came.get((t - 1, f), 1e9))
+                options.append((max(ready, free), t, f, ready))
+            start, t, f, ready = min(options)
+            todo.remove((t, f))
+            free = start + took[f]
+            came[t, f] = free + delay
+            events.append((ready, way, t, f))
+    return sorted(events)
 
 
 def muon_kernel(
@@ -28,6 +56,7 @@
     grad,
     momentum,
     update,
+    momentum_new,
     grad_in,
     momentum_in,
     outgoing,
@@ -36,16 +65,19 @@
     by_source,
     rows,
     squares,
+    turned,
     part,
     send_sum,
     recv_sum,
     strips,
     gram,
     normal,
+    early,
     product,
     done,
     load_sem,
     store_sem,
+    new_sem,
     y_send,
     y_recv,
     x_send,
@@ -86,7 +118,7 @@
     def arrived(ref, sem):
         pltpu.make_async_copy(ref, ref, sem).wait()
 
-    chunks = [turn(z, 4 + t, RING) for t in range(RING)]
+    chunks = [turn(z, j, RING) for j in ORDER]
 
     def columns(q):
         return pl.ds(pl.multiple_of(q * CHUNK, CHUNK), CHUNK)
@@ -135,9 +167,14 @@
         for copy in loads[t]:
             copy.wait()
         q = chunks[t]
+        momentum_in[t][...] = 0.95 * momentum_in[t][...] + grad_in[t][...].astype(jnp.float32)
         for to in range(LOCAL):
-            new = 0.95 * momentum_in[t][chosen[to]] + grad_in[t][chosen[to]].astype(jnp.float32)
-            outgoing[q, to] = new.astype(jnp.bfloat16)
+            outgoing[q, to] = momentum_in[t][chosen[to]].astype(jnp.bfloat16)
+        copy = pltpu.make_async_copy(
+            momentum_in[t], momentum_new.at[:, :, columns(q)], new_sem.at[t]
+        )
+        copy.start()
+        stores.append(copy)
         sent = []
         for to in along_y[1:]:
             copy = remote(
@@ -187,50 +224,41 @@
 
     lane = pl.multiple_of(core * HALF, HALF)
 
-    def make_strip(k):
-        left = rows[k, :, :, pl.ds(lane, HALF)].reshape(2 * OWNED, HALF)
-        for f in range(LOCAL):
-            right = rows[lax.rem(k + core + f, RING)].reshape(2 * OWNED, CHUNK)
-            part[k, :, f * CHUNK : (f + 1) * CHUNK] = lax.dot_general(
-                left, right, (((0,), (0,)), ((), ())), preferred_element_type=jnp.float32
-            )
-        last = lax.rem(k + 4 * (1 - core), RING)
-        right = rows[last, :, :, pl.ds(lane, HALF)].reshape(2 * OWNED, HALF)
-        part[k, :, WIDE:] = lax.dot_general(
-            left, right, (((0,), (0,)), ((), ())), preferred_element_type=jnp.float32
+    def last_lane(which, k):
+        return pl.multiple_of(lax.rem(which + k // LOCAL, 2) * HALF, HALF)
+
+    def make_piece(j, f):
+        k, q = turn(z, j, RING), turn(z, j + f, RING)
+        if f < LOCAL:
+            right = rows[q]
+        else:
+            right = rows[q, :, :, pl.ds(last_lane(core, k), HALF)]
+        part[j, :, COLUMNS[f]] = jnp.dot(
+            turned[j], right.reshape(2 * OWNED, -1), preferred_element_type=jnp.float32
         )
 
     ways = (1, -1)
-    rows_of = [slice(n * PART, (n + 1) * PART) for n in range(PIECES)]
-    half = PIECES // 2
-    order = (tuple(range(half, PIECES)) + tuple(range(half)), tuple(range(PIECES)))
-
-    def from_far(way):
-        return order[way][:half]
-
-    def send_piece(way, t, n):
-        k = turn(z, ways[way] * (4 - t), RING)
-        piece = rows_of[n]
-        value = part[k, piece]
-        if t >= 2 or (t == 1 and n in from_far(way)):
-            arrived(recv_sum.at[way, t - 1, piece], sum_recv.at[way, t - 1, n])
-            value = value + recv_sum[way, t - 1, piece].astype(jnp.float32)
-        send_sum[way, t, piece] = value.astype(jnp.bfloat16)
+
+    def send_piece(way, t, f):
+        j, at = owner(way, t), COLUMNS[f]
+        value = part[j, :, at]
+        if t > 1 or (t == 1 and f in FAR[way]):
+            arrived(recv_sum.at[way, t - 1, :, at], sum_recv.at[way, t - 1, f])
+            value = value + recv_sum[way, t - 1, :, at].astype(jnp.float32)
+        send_sum[way, t, :, at] = value.astype(jnp.bfloat16)
         copy = remote(
-            send_sum.at[way, t, piece],
-            recv_sum.at[way, t, piece],
-            sum_send.at[way, t, n],
-            sum_recv.at[way, t, n],
+            send_sum.at[way, t, :, at],
+            recv_sum.at[way, t, :, at],
+            sum_send.at[way, t, f],
+            sum_recv.at[way, t, f],
             device(x, y, turn(z, ways[way], RING), core),
         )
         copy.start()
         pending.append(copy)
 
-    def send_step(t, which=(0, 1)):
-        for i in range(PIECES if t else half):
-            for way in which:
-                send_piece(way, t, order[way][i])
-
+    sends = plan()
+    total = jnp.zeros((1, CHUNK), jnp.float32)
+    stores = []
     in_flight = [depart(0), depart(1)]
     for t in range(RING + 2):
         if t < RING:
@@ -243,21 +271,17 @@
             share(t - 1)
         if t >= 2:
             shared(t - 2)
-            if t - 2 == 4:
-                make_strip(turn(z, 4, RING))
-                send_step(0)
-            if t - 2 == 5:
-                make_strip(turn(z, -3, RING))
-            if t - 2 == 6:
-                make_strip(turn(z, -2, RING))
-                send_step(1, (1,))
-    make_strip(turn(z, 3, RING))
-    send_step(1, (0,))
-
-    total = jnp.zeros((1, CHUNK), jnp.float32)
-    for q in range(RING):
-        values = rows[q].reshape(2 * OWNED, CHUNK).astype(jnp.float32)
-        total = total + jnp.sum(values * values, axis=0, keepdims=True)
+            q, j = chunks[t - 2], ORDER[t - 2]
+            turned[j] = rows[q, :, :, pl.ds(lane, HALF)].reshape(2 * OWNED, HALF).T
+            for i in ORDER[: t - 1]:
+                for f in range(PIECES):
+                    if (i == j or (i + f) % RING == j) and (i + f) % RING in ORDER[: t - 1]:
+                        make_piece(i, f)
+            while sends and sends[0][0] < t - 0.5:
+                send_piece(*sends.pop(0)[1:])
+            values = rows[q].reshape(2 * OWNED, CHUNK).astype(jnp.float32)
+            total = total + jnp.sum(values * values, axis=0, keepdims=True)
+
     squares[z] = jnp.broadcast_to(total[:, :HALF] + total[:, HALF:], (8, HALF))
     for e in range(1, RING):
         copy = remote(
@@ -270,12 +294,8 @@
         copy.start()
         pending.append(copy)
 
-    make_strip(turn(z, 2, RING))
-    send_step(2)
-    make_strip(turn(z, -1, RING))
-    make_strip(turn(z, 1, RING))
-    send_step(3)
-    make_strip(z)
+    for event in sends:
+        send_piece(*event[1:])
 
     for e in range(1, RING):
         arrived(squares.at[turn(z, -e, RING)], sq_recv.at[e])
@@ -283,23 +303,17 @@
         jnp.sum(squares[:, 0, :], axis=0, keepdims=True), axis=1, keepdims=True
     )
     factor = 0.5 * math.sqrt(FF) / jnp.sqrt(everything + 1e-6)
-    for q in range(RING):
-        normal[:, q * CHUNK : (q + 1) * CHUNK] = (
-            rows[q, core].astype(jnp.float32) * factor
-        ).astype(jnp.bfloat16)
-
-    def spread_piece(way, t, n):
-        k = turn(z, -ways[way] * t, RING)
-        piece = rows_of[n]
+    def spread_piece(way, t, f):
+        k, at = turn(z, -ways[way] * t, RING), COLUMNS[f]
         if t > 0:
-            arrived(strips.at[core, k, piece], all_recv.at[way, t - 1, n])
-        if t == 3 and n not in from_far(way):
+            arrived(strips.at[core, k, :, at], all_recv.at[way, t - 1, f])
+        if t == 3 and f not in FAR[way]:
             return None
         copy = remote(
-            strips.at[core, k, piece],
-            strips.at[core, k, piece],
-            all_send.at[way, t, n],
-            all_recv.at[way, t, n],
+            strips.at[core, k, :, at],
+            strips.at[core, k, :, at],
+            all_send.at[way, t, f],
+            all_recv.at[way, t, f],
             device(x, y, turn(z, ways[way], RING), core),
         )
         copy.start()
@@ -316,78 +330,100 @@
         copy.start()
         pending.append(copy)
 
-    def lay(which, k):
-        at = pl.multiple_of(k * CHUNK + which * HALF, HALF)
-        for f in range(LOCAL):
-            q = lax.rem(k + which + f, RING)
-            block = strips[which, k, :, f * CHUNK : (f + 1) * CHUNK]
-            to = pl.multiple_of(q * CHUNK, CHUNK)
-            gram[pl.ds(at, HALF), pl.ds(to, CHUNK)] = block
-            gram[pl.ds(to, CHUNK), pl.ds(at, HALF)] = block.T
-        q = lax.rem(k + 4 * (1 - which), RING)
-        to = pl.multiple_of(q * CHUNK + which * HALF, HALF)
-        gram[pl.ds(at, HALF), pl.ds(to, HALF)] = strips[which, k, :, WIDE:]
+    def spot(j):
+        return (j + 3) % RING * CHUNK
+
+    def lay(which, j):
+        k = turn(z, j, RING)
+        at = pl.multiple_of(spot(j) + which * HALF, HALF)
+        for f in range(PIECES):
+            to, size = spot(j + f), CHUNK
+            if f == LOCAL:
+                to, size = pl.multiple_of(to + last_lane(which, k), HALF), HALF
+            block = strips[which, k, :, COLUMNS[f]]
+            gram[pl.ds(at, HALF), pl.ds(to, size)] = block
+            if f > 0:
+                gram[pl.ds(to, size), pl.ds(at, HALF)] = block.T
 
     scale = factor * factor
     sent = []
-    for n in range(PIECES):
-        piece = rows_of[n]
+    for f in range(PIECES):
+        at = COLUMNS[f]
         for way in range(2):
-            arrived(recv_sum.at[way, 3, piece], sum_recv.at[way, 3, n])
-        strips[core, z, piece] = (
+            arrived(recv_sum.at[way, 3, :, at], sum_recv.at[way, 3, f])
+        strips[core, z, :, at] = (
             (
-                part[z, piece]
-                + recv_sum[0, 3, piece].astype(jnp.float32)
-                + recv_sum[1, 3, piece].astype(jnp.float32)
+                part[0, :, at]
+                + recv_sum[0, 3, :, at].astype(jnp.float32)
+                + recv_sum[1, 3, :, at].astype(jnp.float32)
             )
             * scale
         ).astype(jnp.bfloat16)
         for way in range(2):
-            sent.append(spread_piece(way, 0, n))
+            sent.append(spread_piece(way, 0, f))
     give_twin(z, 0)
-    lay(core, z)
+    lay(core, 0)
     pending.extend(sent)
 
-    def lay_twin(k, n):
-        arrived(strips.at[1 - core, k], all_twin_recv.at[n])
-        lay(1 - core, k)
-
-    tasks = [lambda: lay_twin(z, 0)]
+    def lay_twin(j, n):
+        arrived(strips.at[1 - core, turn(z, j, RING)], all_twin_recv.at[n])
+        lay(1 - core, j)
+
+    def scale_rows(j):
+        values = rows[turn(z, j, RING), core].astype(jnp.float32)
+        normal[:, spot(j) : spot(j) + CHUNK] = (values * factor).astype(jnp.bfloat16)
+
+    tasks = [functools.partial(scale_rows, j) for j in range(RING)]
+    tasks.append(lambda: lay_twin(0, 0))
     for t in range(1, 4):
         for i in range(PIECES):
             for way in range(2):
-                copy = spread_piece(way, t, order[way][i])
+                copy = spread_piece(way, t, i)
                 if copy is not None:
                     pending.append(copy)
-            if tasks:
-                tasks.pop(0)()
-        below, above = turn(z, -t, RING), turn(z, t, RING)
-        give_twin(below, 2 * t - 1)
-        give_twin(above, 2 * t)
+            for task in tasks[: 2 if t == 1 else 1]:
+                task()
+            tasks = tasks[2 if t == 1 else 1 :]
+        give_twin(turn(z, -t, RING), 2 * t - 1)
+        give_twin(turn(z, t, RING), 2 * t)
         tasks += [
-            functools.partial(lay, core, below),
-            functools.partial(lay, core, above),
-            functools.partial(lay_twin, below, 2 * t - 1),
-            functools.partial(lay_twin, above, 2 * t),
+            functools.partial(lay, core, -t),
+            functools.partial(lay, core, t),
+            functools.partial(lay_twin, -t, 2 * t - 1),
+            functools.partial(lay_twin, t, 2 * t),
         ]
     for task in tasks:
         task()
+
+    near = FF - CHUNK
+
+    def begin(p):
+        early[p] = jnp.dot(
+            normal[:, :near],
+            gram[:near, p * CHUNK : (p + 1) * CHUNK],
+            preferred_element_type=jnp.float32,
+        )
+
+    for p in range(4):
+        begin(p)
     far = turn(z, 4, RING)
     for way in range(2):
-        for n in from_far(way):
-            arrived(strips.at[core, far, rows_of[n]], all_recv.at[way, 3, n])
+        for f in FAR[way]:
+            arrived(strips.at[core, far, :, COLUMNS[f]], all_recv.at[way, 3, f])
     give_twin(far, 7)
-    lay(core, far)
-    lay_twin(far, 7)
-
-    def first(q, carry):
-        at = pl.ds(pl.multiple_of(q * CHUNK, CHUNK), CHUNK)
-        product[:, at] = jnp.dot(
-            normal[...], gram[:, at], preferred_element_type=jnp.float32
-        ).astype(jnp.bfloat16)
-        return carry
-
-    lax.fori_loop(0, RING, first, 0)
+    lay(core, 4)
+    for p in range(4, RING - 1):
+        begin(p)
+    lay_twin(4, 7)
+    for p in range(RING):
+        at = slice(p * CHUNK, (p + 1) * CHUNK)
+        if p < RING - 1:
+            value = early[p] + jnp.dot(
+                normal[:, near:], gram[near:, at], preferred_element_type=jnp.float32
+            )
+        else:
+            value = jnp.dot(normal[...], gram[:, at], preferred_element_type=jnp.float32)
+        product[:, at] = value.astype(jnp.bfloat16)
 
     for q in range(RING):
         at = slice(q * CHUNK, (q + 1) * CHUNK)
@@ -413,14 +449,13 @@
             returned[q].at[x],
             back_recv.at[q, x],
         ).start()
-    stores = []
-    for q in range(RING):
-        at = slice(q * CHUNK, (q + 1) * CHUNK)
+    for p in range(RING):
+        at = columns(turn(z, p + 5, RING))
         for source in range(LOCAL):
-            arrived(returned[q].at[source], back_recv.at[q, source])
+            arrived(returned[p].at[source], back_recv.at[p, source])
         for place in range(LOCAL):
-            placed[place, :, at] = returned[q][origin[place]]
-        copy = pltpu.make_async_copy(placed.at[:, :, at], update.at[:, :, at], store_sem.at[q])
+            placed[place, :, at] = returned[p][origin[place]]
+        copy = pltpu.make_async_copy(placed.at[:, :, at], update.at[:, :, at], store_sem.at[p])
         copy.start()
         stores.append(copy)
     for copy in stores:
@@ -434,13 +469,16 @@
     bf16, f32 = jnp.bfloat16, jnp.float32
     return pl.pallas_call(
         muon_kernel,
-        out_shape=jax.ShapeDtypeStruct((LOCAL, ROWS, FF), bf16),
+        out_shape=[
+            jax.ShapeDtypeStruct((LOCAL, ROWS, FF), bf16),
+            jax.ShapeDtypeStruct((LOCAL, ROWS, FF), f32),
+        ],
         in_specs=[
             pl.BlockSpec(memory_space=pltpu.SMEM),
             pl.BlockSpec(memory_space=pl.ANY),
             pl.BlockSpec(memory_space=pl.ANY),
         ],
-        out_specs=pl.BlockSpec(memory_space=pl.ANY),
+        out_specs=[pl.BlockSpec(memory_space=pl.ANY)] * 2,
         scratch_shapes=[
             [pltpu.VMEM((LOCAL, ROWS, CHUNK), bf16)] * RING,
             [pltpu.VMEM((LOCAL, ROWS, CHUNK), f32)] * RING,
@@ -450,15 +488,18 @@
             pltpu.VMEM((RING, LOCAL, ROWS, CHUNK), bf16),
             pltpu.VMEM((RING, 2, OWNED, CHUNK), bf16),
             pltpu.VMEM((RING, 8, 128), f32),
+            pltpu.VMEM((RING, HALF, 2 * OWNED), bf16),
             pltpu.VMEM((RING, HALF, STRIP), f32),
             pltpu.VMEM((2, 4, HALF, STRIP), bf16),
             pltpu.VMEM((2, 4, HALF, STRIP), bf16),
             pltpu.VMEM((2, RING, HALF, STRIP), bf16),
             pltpu.VMEM((FF, FF), bf16),
             pltpu.VMEM((OWNED, FF), bf16),
+            pltpu.VMEM((RING - 1, OWNED, CHUNK), f32),
             pltpu.VMEM((OWNED, FF), bf16),
             pltpu.VMEM((RING, OWNED, CHUNK), bf16),
             dma((RING, 2)),
+            dma((RING,)),
             dma((RING,)),
             dma((RING, LOCAL)),
             dma((RING, LOCAL)),
@@ -484,9 +525,51 @@
     )(placement, grad, momentum)
 
 
+def settle_kernel(update_from, momentum_from, update, momentum_new, held_update, held, sems):
+    copies = []
+    for j in range(LOCAL):
+        first = [
+            pltpu.make_async_copy(momentum_from.at[j], held.at[j], sems.at[0, j]),
+            pltpu.make_async_copy(update_from.at[j], held_update.at[j], sems.at[1, j]),
+        ]
+        then = [
+            pltpu.make_async_copy(held.at[j], momentum_new.at[j], sems.at[2, j]),
+            pltpu.make_async_copy(held_update.at[j], update.at[j], sems.at[3, j]),
+        ]
+        for copy in first:
+            copy.start()
+        copies.append((first, then))
+    for first, then in copies:
+        for i in range(2):
+            first[i].wait()
+            then[i].start()
+    for _, then in copies:
+        for copy in then:
+            copy.wait()
+
+
+def settle(update, momentum_new):
+    anywhere = pl.BlockSpec(memory_space=pl.ANY)
+    return pl.pallas_call(
+        settle_kernel,
+        out_shape=[
+            jax.ShapeDtypeStruct((LOCAL, ROWS, FF), jnp.bfloat16),
+            jax.ShapeDtypeStruct((LOCAL, ROWS, FF), jnp.float32),
+        ],
+        in_specs=[anywhere] * 2,
+        out_specs=[anywhere] * 2,
+        scratch_shapes=[
+            pltpu.VMEM((LOCAL, ROWS, FF), jnp.bfloat16),
+            pltpu.VMEM((LOCAL, ROWS, FF), jnp.float32),
+            pltpu.SemaphoreType.DMA((4, LOCAL)),
+        ],
+        compiler_params=pltpu.CompilerParams(vmem_limit_bytes=60 << 20),
+        name="settle",
+    )(update, momentum_new)
+
+
 def shards(grad, momentum, placement):
-    update = muon(placement, grad, momentum)
-    momentum_new = 0.95 * momentum + grad.astype(jnp.float32)
+    update, momentum_new = settle(*muon(placement, grad, momentum))
     return (momentum_new, update)
 
 

time: 128 us -> 116 us (0.906)
  Pallas kernels: 122 us -> 115 us
  other arithmetic: 4.29 us -> 0 us
    pallas_call x1 -> x2, Pallas kernels: 122 us -> 115 us  [the longest x1 110 us: muon(): pl.pallas_call(muon_kernel, out_shape=[jax.ShapeDtypeStruct((LOCAL, ROWS,...]
    add x1 -> x0, other arithmetic: 4.29 us -> none  [shards(): momentum_new = 0.95 * momentum + grad.astype(jnp.float32)]
where the time goes in v3:
time: 116 us
  Pallas kernels  115 us (99%)
    pallas_call x1, Pallas kernels, muon(): pl.pallas_call(muon_kernel, out_shape=[jax.ShapeDtypeStruct((LOCAL, ROWS,...  110 us
    pallas_call x1, Pallas kernels, settle(): pl.pallas_call(settle_kernel, out_shape=[jax.ShapeDtypeStruct((LOCAL, ROW...  4.58 us

profile of v3, /device:TPU:1, one launch (start us, length us, event | category | flops | bytes accessed | tf_op | source)
XLA Modules:
  0.0 115.7 jit_solution(15461285839948140697)
XLA Ops:
  0.6 110.3 %muon.1 = (bf16[4,112,2048]{2,1,0:T(8,128)(2,1)}, f32[4,112,2048]{2,1,0:T(8,128)}) custom-call(s32[16]{0:T(128)} %placement.1, bf16[4,112,2048]{2,1,0:T(8,128)(2,1)} %grad.1, f32[4,112,2048]{2,1,0:T(8,128)} %momentum.1), custom_call_target="tpu_custom_call" | custom-call | tf_op jit(solution)/shard_map/muon/pallas_call | solution.py:470
  111.0 4.6 %settle.1 = (bf16[4,112,2048]{2,1,0:T(8,128)(2,1)}, f32[4,112,2048]{2,1,0:T(8,128)}) custom-call(bf16[4,112,2048]{2,1,0:T(8,128)(2,1)} %get-tuple-element.6.update_from, f32[4,112,2048]{2,1,0:T(8,128)} %get-tuple-element.7.momentum_from), custom_call_target="tpu_custom_call" | custom-call | tf_op jit(solution)/shard_map/settle/pallas_call | solution.py:553

commit v4 on v3

--- a/solution.py
+++ b/solution.py
@@ -30,7 +30,7 @@
 
 
 def plan():
-    took, delay = (0.5, 0.5, 0.5, 0.5, 0.25), 0.9
+    took, delay = (0.38, 0.38, 0.38, 0.38, 0.19), 0.7
     events = []
     for way in range(2):
         todo = [(t, f) for t in range(4) for f in range(PIECES) if t or f in FAR[way]]
@@ -146,8 +146,8 @@
         chosen.append(slot)
         origin.append(source)
 
-    along_x = [turn(x, e, LOCAL) for e in range(LOCAL)]
-    along_y = [turn(y, e, LOCAL) for e in range(LOCAL)]
+    along_x = [turn(x, e, LOCAL) for e in (0, 2, 1, 3)]
+    along_y = [turn(y, e, LOCAL) for e in (0, 2, 1, 3)]
     twin = device(x, y, z, 1 - core)
 
     barrier = pltpu.get_barrier_semaphore()
@@ -277,7 +277,7 @@
                 for f in range(PIECES):
                     if (i == j or (i + f) % RING == j) and (i + f) % RING in ORDER[: t - 1]:
                         make_piece(i, f)
-            while sends and sends[0][0] < t - 0.5:
+            while sends and sends[0][0] < t - 0.9:
                 send_piece(*sends.pop(0)[1:])
             values = rows[q].reshape(2 * OWNED, CHUNK).astype(jnp.float32)
             total = total + jnp.sum(values * values, axis=0, keepdims=True)
@@ -425,6 +425,7 @@
             value = jnp.dot(normal[...], gram[:, at], preferred_element_type=jnp.float32)
         product[:, at] = value.astype(jnp.bfloat16)
 
+    early_sends = len(pending)
     for q in range(RING):
         at = slice(q * CHUNK, (q + 1) * CHUNK)
         second = jnp.dot(product[...], gram[:, at], preferred_element_type=jnp.float32)
@@ -449,6 +450,8 @@
             returned[q].at[x],
             back_recv.at[q, x],
         ).start()
+    for copy in pending[:early_sends]:
+        copy.wait_send()
     for p in range(RING):
         at = columns(turn(z, p + 5, RING))
         for source in range(LOCAL):
@@ -460,7 +463,7 @@
         stores.append(copy)
     for copy in stores:
         copy.wait()
-    for copy in pending:
+    for copy in pending[early_sends:]:
         copy.wait_send()
 
 

time: 116 us -> 114 us (0.983)
  Pallas kernels: 115 us -> 112 us
    pallas_call x1, Pallas kernels: 110 us -> 108 us  [muon(): pl.pallas_call(muon_kernel, out_shape=[jax.ShapeDtypeStruct((LOCAL, ROWS,...]
where the time goes in v4:
time: 114 us; the launch traced here: 113 us
  Pallas kernels  112 us (98%)
    pallas_call x1, Pallas kernels, muon(): pl.pallas_call(muon_kernel, out_shape=[jax.ShapeDtypeStruct((LOCAL, ROWS,...  108 us
    pallas_call x1, Pallas kernels, settle(): pl.pallas_call(settle_kernel, out_shape=[jax.ShapeDtypeStruct((LOCAL, ROW...  4.58 us

profile of v4, /device:TPU:1, one launch (start us, length us, event | category | flops | bytes accessed | tf_op | source)
XLA Modules:
  0.0 113.3 jit_solution(15107380316962181508)
XLA Ops:
  0.6 107.9 %muon.1 = (bf16[4,112,2048]{2,1,0:T(8,128)(2,1)}, f32[4,112,2048]{2,1,0:T(8,128)}) custom-call(s32[16]{0:T(128)} %placement.1, bf16[4,112,2048]{2,1,0:T(8,128)(2,1)} %grad.1, f32[4,112,2048]{2,1,0:T(8,128)} %momentum.1), custom_call_target="tpu_custom_call" | custom-call | tf_op jit(solution)/shard_map/muon/pallas_call | solution.py:473
  108.6 4.6 %settle.1 = (bf16[4,112,2048]{2,1,0:T(8,128)(2,1)}, f32[4,112,2048]{2,1,0:T(8,128)}) custom-call(bf16[4,112,2048]{2,1,0:T(8,128)(2,1)} %get-tuple-element.6.update_from, f32[4,112,2048]{2,1,0:T(8,128)} %get-tuple-element.7.momentum_from), custom_call_target="tpu_custom_call" | custom-call | tf_op jit(solution)/shard_map/settle/pallas_call | solution.py:556
